TPU v7x, 32 devices: a whole 2x2x4 slice. The times are simulated.
32 devices in a mesh: clips: 2 (over y), seq: 8 (over z, x), tp: 2 (over core).
Axes of the slice: x: 2, y: 2, z: 4, core: 2. Of those that a mesh axis runs over, the one named last changes fastest.
Arguments:
- video_q: bfloat16 [1024, 2048], P(('clips', 'seq'), 'tp'), parts along dimension 0, may hold values from -30 to 30
- video_k: bfloat16 [1024, 2048], P(('clips', 'seq'), 'tp'), parts along dimension 0, may hold values from -10 to 10
- video_v: bfloat16 [1024, 2048], P(('clips', 'seq'), 'tp'), parts along dimension 0, may hold values from -3 to 3
- audio_q: bfloat16 [256, 1024], P(('clips', 'seq'), 'tp'), parts along dimension 0, may hold values from -30 to 30
- audio_k: bfloat16 [256, 1024], P(('clips', 'seq'), 'tp'), parts along dimension 0, may hold values from -10 to 10
- audio_v: bfloat16 [256, 1024], P(('clips', 'seq'), 'tp'), parts along dimension 0, may hold values from -3 to 3
- video_cross_q: bfloat16 [1024, 1024], P(('clips', 'seq'), 'tp'), parts along dimension 0, may hold values from -40 to 40
- audio_cross_q: bfloat16 [256, 2048], P(('clips', 'seq'), 'tp'), parts along dimension 0, may hold values from -40 to 40
- audio_key_gain: float32 [64], replicated, may hold values from 0.5 to 2
- video_key_gain: float32 [128], replicated, may hold values from 0.5 to 2
Outputs:
- video_self: bfloat16 [1024, 2048], P(('clips', 'seq'), 'tp'), parts along dimension 0
- audio_self: bfloat16 [256, 1024], P(('clips', 'seq'), 'tp'), parts along dimension 0
- video_cross: bfloat16 [1024, 1024], P(('clips', 'seq'), 'tp'), parts along dimension 0
- audio_cross: bfloat16 [256, 2048], P(('clips', 'seq'), 'tp'), parts along dimension 0
There are 2 independent parts, one for each index of `clips`. A program takes and returns all parts, laid end to end along the dimension named above; an argument that names none is the same for every part. Nothing has to cross between parts.
All inputs are finite; a program needn't handle non-finite values.
Results may differ from a plain program's by a relative error of at most 0.011.
Values may be sent and summed in bfloat16 or wider, within the bound.
A program may use at most 128 MiB of HBM per device.

v0:
```python
import math

import jax
import jax.numpy as jnp
from jax import lax
from jax.sharding import PartitionSpec as P

VHEAD = 128
AHEAD = 64


def split_heads(matrix, head_size):
    return matrix.reshape(matrix.shape[0], matrix.shape[1] // head_size, head_size)


def block_scores(queries, key_rows, head_size):
    products = jnp.einsum(
        "qhd,khd->hqk",
        split_heads(queries, head_size),
        split_heads(key_rows, head_size),
        preferred_element_type=jnp.float32,
    )
    return products * (1.0 / math.sqrt(head_size))


def blank_state(queries, head_size):
    head_count = queries.shape[1] // head_size
    row_count = queries.shape[0]
    return (
        jnp.full((head_count, row_count), -jnp.inf, jnp.float32),
        jnp.zeros((head_count, row_count), jnp.float32),
        jnp.zeros((head_count, row_count, head_size), jnp.float32),
    )


def absorb(state, queries, key_rows, value_rows, head_size):
    maxima, totals, summed = state
    scores = block_scores(queries, key_rows, head_size)
    raised = jnp.max(scores, axis=2)
    shrink = jnp.exp(maxima - raised)
    weights = jnp.exp(scores - raised[:, :, None])
    totals = totals * shrink + jnp.sum(weights, axis=2)
    update = jnp.einsum(
        "hqk,khd->hqd",
        weights.astype(jnp.bfloat16),
        split_heads(value_rows, head_size),
        preferred_element_type=jnp.float32,
    )
    summed = summed * shrink[:, :, None] + update
    return (raised, totals, summed)


def finish(state):
    maxima, totals, summed = state
    output = summed / totals[:, :, None]
    return jnp.transpose(output, (1, 0, 2)).reshape(output.shape[1], -1).astype(jnp.bfloat16)


def cross_keys(states, gain_vector, head_size):
    values = split_heads(states, head_size).astype(jnp.float32)
    factor = lax.rsqrt(jnp.mean(values * values, axis=2, keepdims=True) + 1e-06)
    return (values * factor * gain_vector).astype(jnp.bfloat16).reshape(states.shape)


def shards(
    video_q,
    video_k,
    video_v,
    audio_q,
    audio_k,
    audio_v,
    video_cross_q,
    audio_cross_q,
    audio_key_gain,
    video_key_gain,
):
    pieces = (
        lax.all_gather(audio_k, "seq", axis=0, tiled=True),
        lax.all_gather(audio_v, "seq", axis=0, tiled=True),
    )
    audio_state = absorb(blank_state(audio_q, AHEAD), audio_q, pieces[0], pieces[1], AHEAD)
    audio_self = finish(audio_state)
    audio_whole = lax.all_gather(audio_self, "seq", axis=0, tiled=True)
    audio_normed = cross_keys(audio_whole, audio_key_gain, AHEAD)
    video_cross = finish(
        absorb(blank_state(video_cross_q, AHEAD), video_cross_q, audio_normed, audio_whole, AHEAD)
    )
    pieces = (
        lax.all_gather(video_k, "seq", axis=0, tiled=True),
        lax.all_gather(video_v, "seq", axis=0, tiled=True),
    )
    video_state = absorb(blank_state(video_q, VHEAD), video_q, pieces[0], pieces[1], VHEAD)
    video_self = finish(video_state)
    pieces = lax.all_gather(video_self, "seq", axis=0, tiled=True)
    cross_state = absorb(
        blank_state(audio_cross_q, VHEAD),
        audio_cross_q,
        cross_keys(pieces, video_key_gain, VHEAD),
        pieces,
        VHEAD,
    )
    audio_cross = finish(cross_state)
    return (video_self, audio_self, video_cross, audio_cross)


def solution(mesh):
    return jax.shard_map(
        shards,
        mesh=mesh,
        in_specs=(
            P(("clips", "seq"), "tp"),
            P(("clips", "seq"), "tp"),
            P(("clips", "seq"), "tp"),
            P(("clips", "seq"), "tp"),
            P(("clips", "seq"), "tp"),
            P(("clips", "seq"), "tp"),
            P(("clips", "seq"), "tp"),
            P(("clips", "seq"), "tp"),
            P(),
            P(),
        ),
        out_specs=(
            P(("clips", "seq"), "tp"),
            P(("clips", "seq"), "tp"),
            P(("clips", "seq"), "tp"),
            P(("clips", "seq"), "tp"),
        ),
        check_vma=False,
    )
```

profile of v0, /device:TPU:0, one launch (start us, length us, event | category | flops | bytes accessed | tf_op | source)
XLA Modules:
  0.0 147.3 jit_solution(8551850040109692584)
XLA Ops:
  7.2 0.7 all-gather.4.cloned.1.call-update
  8.0 0.7 all-gather.6.cloned.1.call-update
  8.7 0.8 reshape.113
  9.5 32.7 %all_gather.20 = bf16[128,512]{1,0:T(8,128)(2,1)S(1)} all-gather(bf16[16,512]{1,0:T(8,128)(2,1)} %param.14), channel_id=1, replica_groups=mesh['clips'=2,'seq'=8,'tp'=2] {'seq'}, dimensions={0}, use_global_device_ids=true | all-gather | bytes 147456 | tf_op jit(solution)/shard_map/all_gather | solution.py:78
  42.4 31.2 %all_gather.21 = bf16[128,512]{1,0:T(8,128)(2,1)S(1)} all-gather(bf16[16,512]{1,0:T(8,128)(2,1)} %param.15), channel_id=1, replica_groups=mesh['clips'=2,'seq'=8,'tp'=2] {'seq'}, dimensions={0}, use_global_device_ids=true | all-gather | bytes 147456 | tf_op jit(solution)/shard_map/all_gather | solution.py:79
  74.1 1.5 %copy.39 = bf16[512,1024]{0,1:T(8,128)(2,1)S(1)} copy(bf16[512,1024]{1,0:T(8,128)(2,1)} %all-gather.4.cloned.1.call-done) | data formatting | bytes 2097152 | tf_op jit(solution)/shard_map/all_gather | solution.py:89
  75.6 0.4 fusion.50
  76.0 0.4 fusion.22
  76.4 18.2 %all-gather.6.cloned.1.call-done = bf16[512,1024]{1,0:T(8,128)(2,1)} async-done(((bf16[64,1024]{1,0:T(8,128)(2,1)}), bf16[512,1024]{1,0:T(8,128)(2,1)}) %all-gather.6.cloned.1.call-update) | async-done | bytes 1048592 | tf_op jit(solution)/shard_map/all_gather | solution.py:90
  94.7 1.5 %copy.42 = bf16[512,1024]{0,1:T(8,128)(2,1)S(1)} copy(bf16[512,1024]{1,0:T(8,128)(2,1)} %all-gather.6.cloned.1.call-done) | data formatting | bytes 2097152 | tf_op jit(solution)/shard_map/all_gather | solution.py:90
  96.2 0.5 fusion.11
  96.7 0.7 copy.87
  97.4 0.2 fusion.16
  97.8 31.1 %all_gather.22 = bf16[128,512]{1,0:T(8,128)(2,1)S(1)} all-gather(bf16[16,512]{1,0:T(8,128)(2,1)S(1)} %convert_element_type.53), channel_id=1, replica_groups=mesh['clips'=2,'seq'=8,'tp'=2] {'seq'}, dimensions={0}, use_global_device_ids=true | all-gather | bytes 147456 | tf_op jit(solution)/shard_map/all_gather | solution.py:83
  129.2 0.3 fusion.52
  129.6 0.3 fusion.29
  129.9 0.3 fusion.9
  130.3 0.8 convert_element_type.58
  131.1 5.7 %all-gather.8.cloned.1.call-done = bf16[512,1024]{1,0:T(8,128)(2,1)} async-done(((bf16[64,1024]{1,0:T(8,128)(2,1)}), bf16[512,1024]{1,0:T(8,128)(2,1)}) %all-gather.8.cloned.1.call-update) | async-done | bytes 1048592 | tf_op jit(solution)/shard_map/all_gather | solution.py:94
  136.8 1.5 %copy.52 = bf16[512,1024]{0,1:T(8,128)(2,1)S(1)} copy(bf16[512,1024]{1,0:T(8,128)(2,1)} %all-gather.8.cloned.1.call-done) | data formatting | bytes 2097152 | tf_op jit(solution)/shard_map/all_gather | solution.py:94
  138.6 0.5 copy-done.3
  139.1 0.5 fusion.53
  139.7 0.4 fusion.18
  140.2 0.6 copy.88
  (38 shorter events, 1.8 us)
Async XLA Ops:
  7.2 68.5 %copy-start = (bf16[64,1024]{1,0:T(8,128)(2,1)S(1)}, bf16[64,1024]{1,0:T(8,128)(2,1)}, u32[]{:S(2)}) copy-start(bf16[64,1024]{1,0:T(8,128)(2,1)} %param.10) | copy-start | bytes 393220
  7.2 66.9 %all-gather.4.cloned.1.call-start = ((), (), s32[]{:S(2)}) async-start(), calls=%async_computation | async-start | bytes 1179648 | tf_op jit(solution)/shard_map/all_gather | solution.py:89
  7.9 86.7 %all-gather.6.cloned.1.call-start = ((), (), s32[]{:S(2)}) async-start(), calls=%async_computation.1 | async-start | bytes 1179648 | tf_op jit(solution)/shard_map/all_gather | solution.py:90
  8.7 128.1 %all-gather.8.cloned.1.call-start = ((), (), s32[]{:S(2)}) async-start(), calls=%async_computation.2 | async-start | bytes 1179648 | tf_op jit(solution)/shard_map/all_gather | solution.py:94
  96.7 32.3 %copy-start.1 = (bf16[64,512]{1,0:T(8,128)(2,1)S(1)}, bf16[64,512]{1,0:T(8,128)(2,1)}, u32[]{:S(2)}) copy-start(bf16[64,512]{1,0:T(8,128)(2,1)} %param.16) | copy-start | bytes 196612
  96.7 32.5 %copy-start.4 = (f32[64]{0:T(128)S(1)}, f32[64]{0:T(128)}, u32[]{:S(2)}) copy-start(f32[64]{0:T(128)} %param.18) | copy-start | bytes 772
  97.8 32.4 %copy-start.2 = (bf16[16,512]{1,0:T(8,128)(2,1)}, bf16[16,512]{1,0:T(8,128)(2,1)S(1)}, u32[]{:S(2)}) copy-start(bf16[16,512]{1,0:T(8,128)(2,1)S(1)} %convert_element_type.53) | copy-start | bytes 49156
  138.3 0.8 copy-start.3
  138.3 0.8 copy-start.5
Sparse Core Ops, SparseCore 0:
  10.1 43.1 all-gather.3
  55.5 39.1 all-gather.5
  97.5 39.2 all-gather.7
where the time goes:
time: 148 us; the launch traced here: 147 us
  blocking collectives  95 us (64%)
  waiting for transfers between devices  25.4 us (17%)
  between operations  14 us (9%)
  local copies, waits for them, and re-layouts  8.59 us (6%)
  matrix products  2.87 us (2%)
    all_gather x1, blocking collectives, shards(): lax.all_gather(audio_k, 'seq', axis=0, tiled=True)  32.7 us
    all_gather x1, blocking collectives, shards(): lax.all_gather(audio_v, 'seq', axis=0, tiled=True)  31.2 us
    all_gather x1, blocking collectives, shards(): audio_whole = lax.all_gather(audio_self, 'seq', axis=0, tiled=True)  31.1 us
    all_gather x1, waiting for transfers between devices, shards(): lax.all_gather(video_v, 'seq', axis=0, tiled=True)  18.2 us
    all_gather x1, waiting for transfers between devices, shards(): pieces = lax.all_gather(video_self, 'seq', axis=0, tiled=True)  5.72 us
  transfers between devices with their start and end apart: 3, of which 2 were waited for; matrix products, arithmetic and copies ran while one was open for 4% of the time, Pallas kernels for 0%

commit v1 on v0

v1 whole, which is shorter than its diff:
```python
import functools
import math

import jax
import jax.numpy as jnp
from jax import lax
from jax.experimental import pallas as pl
from jax.experimental.pallas import tpu as pltpu
from jax.sharding import PartitionSpec as P

VHEAD = 128
AHEAD = 64
LANES = 128
LOG2E = math.log2(math.e)


def split_heads(matrix, head_size):
    return matrix.reshape(matrix.shape[0], matrix.shape[1] // head_size, head_size)


def attend(queries, key_rows, value_rows, head_size):
    scores = jnp.einsum(
        "qhd,khd->hqk",
        split_heads(queries, head_size),
        split_heads(key_rows, head_size),
        preferred_element_type=jnp.float32,
    ) * (1.0 / math.sqrt(head_size))
    weights = jnp.exp(scores - jnp.max(scores, axis=2, keepdims=True))
    totals = jnp.sum(weights, axis=2)
    summed = jnp.einsum(
        "hqk,khd->hqd",
        weights.astype(jnp.bfloat16),
        split_heads(value_rows, head_size),
        preferred_element_type=jnp.float32,
    )
    output = summed / totals[:, :, None]
    return jnp.transpose(output, (1, 0, 2)).reshape(output.shape[1], -1).astype(jnp.bfloat16)


def cross_keys(states, gain_vector, head_size):
    values = split_heads(states, head_size).astype(jnp.float32)
    factor = lax.rsqrt(jnp.mean(values * values, axis=2, keepdims=True) + 1e-06)
    return (values * factor * gain_vector).astype(jnp.bfloat16).reshape(states.shape)


def gathered_shards(
    video_q, video_k, video_v, audio_q, audio_k, audio_v,
    video_cross_q, audio_cross_q, audio_key_gain, video_key_gain,
):
    def whole(x):
        return lax.all_gather(x, "seq", axis=0, tiled=True)

    audio_self = attend(audio_q, whole(audio_k), whole(audio_v), AHEAD)
    audio_whole = whole(audio_self)
    video_cross = attend(
        video_cross_q, cross_keys(audio_whole, audio_key_gain, AHEAD), audio_whole, AHEAD
    )
    video_self = attend(video_q, whole(video_k), whole(video_v), VHEAD)
    video_whole = whole(video_self)
    audio_cross = attend(
        audio_cross_q, cross_keys(video_whole, video_key_gain, VHEAD), video_whole, VHEAD
    )
    return (video_self, audio_self, video_cross, audio_cross)


def dot_t(a, b):
    return lax.dot_general(a, b, (((1,), (1,)), ((), ())), preferred_element_type=jnp.float32)


def soft(scores, head_size):
    top = jnp.max(scores, axis=1, keepdims=True)
    e = jnp.exp2((scores - top) * (LOG2E / math.sqrt(head_size)))
    return e.astype(jnp.bfloat16), 1.0 / jnp.sum(e, axis=1, keepdims=True)


def one_head(q, k, v):
    w, inv = soft(dot_t(q, k), VHEAD)
    return (jnp.dot(w, v, preferred_element_type=jnp.float32) * inv).astype(jnp.bfloat16)


def head_pair(q, k, v, low):
    zero = jnp.zeros_like(q)
    lowq = low[: q.shape[0]]
    wa, ia = soft(dot_t(jnp.where(lowq, q, zero), k), AHEAD)
    wb, ib = soft(dot_t(jnp.where(lowq, zero, q), k), AHEAD)
    oa = jnp.dot(wa, v, preferred_element_type=jnp.float32) * ia
    ob = jnp.dot(wb, v, preferred_element_type=jnp.float32) * ib
    return jnp.where(lowq, oa, ob).astype(jnp.bfloat16)


def kernel(
    n, vt, at,
    vq, vk, vv, aq, ak, av, vcq, acq, again, vgain,
    o_vs, o_as, o_vc, o_ac,
    vstage, astage, cstage, vrecv, arecv, crecv, vs_buf, as_buf, vc_buf, ac_buf,
    stage_sem, send_sem, recv_sem,
):
    me = lax.axis_index("seq")
    half = n // 2
    my_half = me // half
    my_pair = lax.rem(me, half)
    kv_rows, v_rows = 2 * vt, 3 * vt + at
    KV, QA, AU, CQ, OVS, OAS, OVC, OAC = range(8)

    stages = [
        (vk, vstage.at[pl.ds(0, vt)]),
        (vv, vstage.at[pl.ds(vt, vt)]),
        (vq, vstage.at[pl.ds(2 * vt, vt)]),
        (acq, vstage.at[pl.ds(3 * vt, at)]),
        (aq, astage.at[pl.ds(0, at)]),
        (ak, astage.at[pl.ds(at, at)]),
        (av, astage.at[pl.ds(2 * at, at)]),
        (vcq, cstage),
    ]
    stages = [pltpu.make_async_copy(s, d, stage_sem.at[i]) for i, (s, d) in enumerate(stages)]
    for c in stages:
        c.start()

    barrier = pltpu.get_barrier_semaphore()
    for k in range(1, n):
        pl.semaphore_signal(
            barrier, inc=1, device_id={"seq": lax.rem(me + k, n)},
            device_id_type=pl.DeviceIdType.MESH,
        )
    for c in stages:
        c.wait()
    pl.semaphore_wait(barrier, n - 1)

    order = sorted(range(1, n), key=lambda k: abs(k - half))
    near = list(range(1, half))

    def lanes(ref, rows, block):
        return ref.at[rows, pl.ds(pl.multiple_of(block * LANES, LANES), LANES)]

    def remote(src, dst, kind, peer):
        pltpu.make_async_remote_copy(
            src_ref=src, dst_ref=dst, send_sem=send_sem.at[kind], recv_sem=recv_sem.at[kind],
            device_id={"seq": peer}, device_id_type=pl.DeviceIdType.MESH,
        ).start()

    def local(src, dst, kind):
        pltpu.make_async_copy(src, dst, recv_sem.at[kind]).start()

    def drain(ref, sem):
        pltpu.make_async_copy(ref, ref, sem).wait()

    everyone = [lax.rem(me + k, n) for k in order]
    halfmates = [my_half * half + lax.rem(my_pair + k, half) for k in near]

    kv, qa = pl.ds(0, kv_rows), pl.ds(kv_rows, v_rows - kv_rows)
    for rows, kind in ((kv, KV), (qa, QA)):
        for peer in everyone:
            remote(lanes(vstage, rows, peer), vrecv.at[me, rows], kind, peer)
        local(lanes(vstage, rows, me), vrecv.at[me, rows], kind)
    for peer in everyone:
        remote(lanes(astage, slice(None), lax.rem(peer, half)), arecv.at[me], AU, peer)
    local(lanes(astage, slice(None), my_pair), arecv.at[me], AU)
    for peer in halfmates:
        remote(lanes(cstage, slice(None), lax.rem(peer, half)), crecv.at[my_pair], CQ, peer)
    local(lanes(cstage, slice(None), my_pair), crecv.at[my_pair], CQ)

    drain(vrecv.at[:, kv], recv_sem.at[KV])
    drain(vrecv.at[:, qa], recv_sem.at[QA])
    key_rows = vrecv[:, :vt].reshape(n * vt, VHEAD)
    value_rows = vrecv[:, vt : 2 * vt].reshape(n * vt, VHEAD)
    for i in range(0, n, 2):
        q = vrecv[i : i + 2, 2 * vt : 3 * vt].reshape(2 * vt, VHEAD)
        vs_buf[i : i + 2] = one_head(q, key_rows, value_rows).reshape(2, vt, VHEAD)
    for peer in everyone:
        remote(vs_buf.at[peer], lanes(o_vs, slice(None), me), OVS, peer)
    local(vs_buf.at[me], lanes(o_vs, slice(None), me), OVS)

    states = vs_buf[...].reshape(n * vt, VHEAD)
    x = states.astype(jnp.float32)
    factor = lax.rsqrt(jnp.sum(x * x, axis=1, keepdims=True) * (1.0 / VHEAD) + 1e-06)
    normed = (x * factor * vgain[...]).astype(jnp.bfloat16)
    q = vrecv[:, 3 * vt :].reshape(n * at, VHEAD)
    ac_buf[...] = one_head(q, normed, states).reshape(n, at, VHEAD)
    for peer in everyone:
        remote(ac_buf.at[peer], lanes(o_ac, slice(None), me), OAC, peer)
    local(ac_buf.at[me], lanes(o_ac, slice(None), me), OAC)

    drain(arecv, recv_sem.at[AU])
    low = lax.broadcasted_iota(jnp.int32, (half * vt, LANES), 1) < AHEAD
    states = head_pair(
        arecv[:, :at].reshape(n * at, LANES),
        arecv[:, at : 2 * at].reshape(n * at, LANES),
        arecv[:, 2 * at :].reshape(n * at, LANES),
        low,
    )
    as_buf[...] = states.reshape(n, at, LANES)
    for peer in halfmates:
        remote(as_buf.at[peer], lanes(o_as, slice(None), my_pair), OAS, peer)
    local(as_buf.at[me], lanes(o_as, slice(None), my_pair), OAS)

    x = states.astype(jnp.float32)
    lowx = low[: n * at]
    square = x * x
    zero = jnp.zeros_like(square)
    means = jnp.where(
        lowx,
        jnp.sum(jnp.where(lowx, square, zero), axis=1, keepdims=True),
        jnp.sum(jnp.where(lowx, zero, square), axis=1, keepdims=True),
    ) * (1.0 / AHEAD)
    gain = jnp.concatenate([again[...], again[...]], axis=1)
    normed = (x * lax.rsqrt(means + 1e-06) * gain).astype(jnp.bfloat16)
    drain(crecv, recv_sem.at[CQ])
    q = crecv[...].reshape(half * vt, LANES)
    vc_buf[...] = head_pair(q, normed, states, low).reshape(half, vt, LANES)
    for peer in halfmates:
        remote(vc_buf.at[lax.rem(peer, half)], lanes(o_vc, slice(None), my_pair), OVC, peer)
    local(vc_buf.at[my_pair], lanes(o_vc, slice(None), my_pair), OVC)

    far, mates = pl.ds(0, n - 1), pl.ds(0, half - 1)
    drain(vrecv.at[far, kv], send_sem.at[KV])
    drain(vrecv.at[far, qa], send_sem.at[QA])
    drain(arecv.at[far], send_sem.at[AU])
    drain(crecv.at[mates], send_sem.at[CQ])
    drain(vs_buf.at[far], send_sem.at[OVS])
    drain(ac_buf.at[far], send_sem.at[OAC])
    drain(as_buf.at[mates], send_sem.at[OAS])
    drain(vc_buf.at[mates], send_sem.at[OVC])
    drain(o_vs, recv_sem.at[OVS])
    drain(o_as, recv_sem.at[OAS])
    drain(o_vc, recv_sem.at[OVC])
    drain(o_ac, recv_sem.at[OAC])


def exchanged_shards(
    n, video_q, video_k, video_v, audio_q, audio_k, audio_v,
    video_cross_q, audio_cross_q, audio_key_gain, video_key_gain,
):
    vt, at = video_q.shape[0], audio_q.shape[0]
    half = n // 2
    bf = jnp.bfloat16
    anywhere = pl.BlockSpec(memory_space=pl.ANY)
    vmem = pl.BlockSpec(memory_space=pltpu.VMEM)
    outs = [video_q, audio_q, video_cross_q, audio_cross_q]
    return pl.pallas_call(
        functools.partial(kernel, n, vt, at),
        out_shape=[jax.ShapeDtypeStruct(x.shape, bf) for x in outs],
        in_specs=[anywhere] * 8 + [vmem] * 2,
        out_specs=[anywhere] * 4,
        scratch_shapes=[
            pltpu.VMEM((3 * vt + at, video_q.shape[1]), bf),
            pltpu.VMEM((3 * at, audio_q.shape[1]), bf),
            pltpu.VMEM((vt, video_cross_q.shape[1]), bf),
            pltpu.VMEM((n, 3 * vt + at, LANES), bf),
            pltpu.VMEM((n, 3 * at, LANES), bf),
            pltpu.VMEM((half, vt, LANES), bf),
            pltpu.VMEM((n, vt, LANES), bf),
            pltpu.VMEM((n, at, LANES), bf),
            pltpu.VMEM((half, vt, LANES), bf),
            pltpu.VMEM((n, at, LANES), bf),
            pltpu.SemaphoreType.DMA((8,)),
            pltpu.SemaphoreType.DMA((8,)),
            pltpu.SemaphoreType.DMA((8,)),
        ],
        compiler_params=pltpu.CompilerParams(
            collective_id=0, has_side_effects=True, vmem_limit_bytes=32 * 2**20
        ),
    )(
        video_q, video_k, video_v, audio_q, audio_k, audio_v, video_cross_q, audio_cross_q,
        audio_key_gain.reshape(1, AHEAD), video_key_gain.reshape(1, VHEAD),
    )


def solution(mesh):
    n = mesh.shape["seq"]

    def shards(*args):
        video_heads = args[0].shape[1] // VHEAD
        audio_pairs = args[3].shape[1] // (2 * AHEAD)
        if video_heads == n and 2 * audio_pairs == n:
            return tuple(exchanged_shards(n, *args))
        return gathered_shards(*args)

    split = P(("clips", "seq"), "tp")
    return jax.shard_map(
        shards,
        mesh=mesh,
        in_specs=(split,) * 8 + (P(), P()),
        out_specs=(split,) * 4,
        check_vma=False,
    )
```

time: 148 us -> 36.4 us (0.25)
  blocking collectives: 95 us -> 0 us
  Pallas kernels: 0 us -> 25.6 us
  waiting for transfers between devices: 25.4 us -> 0 us
  between operations: 14 us -> 0.67 us
  matrix products: 2.87 us -> 0 us
    all_gather x3 -> x0, blocking collectives: 95 us -> none  [the longest x1 32.7 us: shards(): lax.all_gather(audio_k, 'seq', axis=0, tiled=True)]
    pallas_call x0 -> x1, Pallas kernels: none -> 25.6 us  [exchanged_shards(): pl.pallas_call(functools.partial(kernel, n, vt, at), out_shape=[jax.Shape...]
    all_gather x3 -> x0, waiting for transfers between devices: 24 us -> none  [the longest x1 18.2 us: shards(): lax.all_gather(video_v, 'seq', axis=0, tiled=True)]
    unnamed x12 -> x24, local copies, waits for them, and re-layouts: 0.52 us -> 9.62 us
    all_gather x6 -> x0, local copies, waits for them, and re-layouts: 4.83 us -> none  [the longest x1 1.5 us: shards(): lax.all_gather(video_k, 'seq', axis=0, tiled=True)]
    dot_general x8 -> x0, matrix products: 2.87 us -> none  [the longest x4 1.46 us: absorb(): jnp.einsum('hqk,khd->hqd', weights.astype(jnp.bfloat16), split_heads(valu...]
    convert_element_type x6 -> x0, local copies, waits for them, and re-layouts: 2.3 us -> none  [finish(): jnp.transpose(output, (1, 0, 2)).reshape(output.shape[1], -1)]
  transfers between devices with their start and end apart: 3 -> 0, of which waited for: 2 -> 0; matrix products, arithmetic and copies ran while one was open for 4% -> 0% of each run, Pallas kernels for 0% -> 0%
where the time goes in v1:
time: 36.4 us; the launch traced here: 35.9 us
  Pallas kernels  25.6 us (70%)
  local copies, waits for them, and re-layouts  9.62 us (26%)
  between operations  0.67 us (2%)
    pallas_call x1, Pallas kernels, exchanged_shards(): pl.pallas_call(functools.partial(kernel, n, vt, at), out_shape=[jax.Shape...  25.6 us
    unnamed x24, local copies, waits for them, and re-layouts  9.62 us

profile of v1, /device:TPU:0, one launch (start us, length us, event | category | flops | bytes accessed | tf_op | source)
XLA Modules:
  0.0 35.9 jit_solution(1573898174023464285)
XLA Ops:
  0.6 0.0 copy-start.8
  0.6 0.0 copy-start.9
  0.7 0.6 %copy-done.8 = f32[64]{0:T(128)S(1)} copy-done((f32[64]{0:T(128)S(1)}, f32[64]{0:T(128)}, u32[]{:S(2)}) %copy-start.8) | copy-done | bytes 280
  1.3 0.0 copy-done.9
  1.3 0.0 copy-start
  1.3 0.9 %copy-done = bf16[64,1024]{1,0:T(8,128)(2,1)S(1)} copy-done((bf16[64,1024]{1,0:T(8,128)(2,1)S(1)}, bf16[64,1024]{1,0:T(8,128)(2,1)}, u32[]{:S(2)}) %copy-start) | copy-done | bytes 131096
  2.2 0.0 copy-start.1
  2.2 0.9 %copy-done.1 = bf16[64,1024]{1,0:T(8,128)(2,1)S(1)} copy-done((bf16[64,1024]{1,0:T(8,128)(2,1)S(1)}, bf16[64,1024]{1,0:T(8,128)(2,1)}, u32[]{:S(2)}) %copy-start.1) | copy-done | bytes 131096
  3.1 0.0 copy-start.2
  3.1 0.9 %copy-done.2 = bf16[64,1024]{1,0:T(8,128)(2,1)S(1)} copy-done((bf16[64,1024]{1,0:T(8,128)(2,1)S(1)}, bf16[64,1024]{1,0:T(8,128)(2,1)}, u32[]{:S(2)}) %copy-start.2) | copy-done | bytes 131096
  4.0 0.0 copy-start.3
  4.0 0.8 %copy-done.3 = bf16[64,512]{1,0:T(8,128)(2,1)S(1)} copy-done((bf16[64,512]{1,0:T(8,128)(2,1)S(1)}, bf16[64,512]{1,0:T(8,128)(2,1)}, u32[]{:S(2)}) %copy-start.3) | copy-done | bytes 65560
  4.9 0.0 copy-start.4
  4.9 0.8 %copy-done.4 = bf16[16,1024]{1,0:T(8,128)(2,1)S(1)} copy-done((bf16[16,1024]{1,0:T(8,128)(2,1)S(1)}, bf16[16,1024]{1,0:T(8,128)(2,1)}, u32[]{:S(2)}) %copy-start.4) | copy-done | bytes 32792
  5.6 0.0 copy-start.5
  5.6 0.7 %copy-done.5 = bf16[16,512]{1,0:T(8,128)(2,1)S(1)} copy-done((bf16[16,512]{1,0:T(8,128)(2,1)S(1)}, bf16[16,512]{1,0:T(8,128)(2,1)}, u32[]{:S(2)}) %copy-start.5) | copy-done | bytes 16408
  6.3 0.0 copy-start.6
  6.3 0.7 %copy-done.6 = bf16[16,512]{1,0:T(8,128)(2,1)S(1)} copy-done((bf16[16,512]{1,0:T(8,128)(2,1)S(1)}, bf16[16,512]{1,0:T(8,128)(2,1)}, u32[]{:S(2)}) %copy-start.6) | copy-done | bytes 16408
  7.1 0.7 %copy-done.7 = bf16[16,512]{1,0:T(8,128)(2,1)S(1)} copy-done((bf16[16,512]{1,0:T(8,128)(2,1)S(1)}, bf16[16,512]{1,0:T(8,128)(2,1)}, u32[]{:S(2)}) %copy-start.7) | copy-done | bytes 16408
  7.8 25.6 %shard_map.129 = (bf16[64,1024]{1,0:T(8,128)(2,1)S(1)}, bf16[16,512]{1,0:T(8,128)(2,1)S(1)}, bf16[64,512]{1,0:T(8,128)(2,1)S(1)}, bf16[16,1024]{1,0:T(8,128)(2,1)S(1)}) custom-call(bf16[64,1024]{1,0:T(8,128)(2,1)S(1)} %copy-done, bf16[64,1024]{1,0:T(8,128)(2,1)S(1)} %copy-done.1, bf16[64,1024]{1,0:T(8,128)(2,1)S(1)} %copy-done.2, ...), custom_call_target="tpu_custom_call" | custom-call | tf_op jit(solution)/shard_map/pallas_call | solution.py:239
  33.4 0.7 %copy.18 = bf16[64,1024]{1,0:T(8,128)(2,1)} copy(bf16[64,1024]{1,0:T(8,128)(2,1)S(1)} %get-tuple-element.8) | data formatting | bytes 262144
  34.1 0.6 %copy.19 = bf16[16,512]{1,0:T(8,128)(2,1)} copy(bf16[16,512]{1,0:T(8,128)(2,1)S(1)} %get-tuple-element.9) | data formatting | bytes 32768
  34.7 0.6 %copy.20 = bf16[64,512]{1,0:T(8,128)(2,1)} copy(bf16[64,512]{1,0:T(8,128)(2,1)S(1)} %get-tuple-element.10) | data formatting | bytes 131072
  35.3 0.6 %copy.21 = bf16[16,1024]{1,0:T(8,128)(2,1)} copy(bf16[16,1024]{1,0:T(8,128)(2,1)S(1)} %get-tuple-element.11) | data formatting | bytes 65536
  (1 shorter events, 0.0 us)
Async XLA Ops:
  0.6 0.7 %copy-start.8 = (f32[64]{0:T(128)S(1)}, f32[64]{0:T(128)}, u32[]{:S(2)}) copy-start(f32[64]{0:T(128)} %param.18) | copy-start | bytes 772
  0.6 0.7 %copy-start.9 = (f32[128]{0:T(128)S(1)}, f32[128]{0:T(128)}, u32[]{:S(2)}) copy-start(f32[128]{0:T(128)} %param.19) | copy-start | bytes 1540
  1.3 0.9 %copy-start = (bf16[64,1024]{1,0:T(8,128)(2,1)S(1)}, bf16[64,1024]{1,0:T(8,128)(2,1)}, u32[]{:S(2)}) copy-start(bf16[64,1024]{1,0:T(8,128)(2,1)} %vq.1) | copy-start | bytes 393220
  2.2 0.9 %copy-start.1 = (bf16[64,1024]{1,0:T(8,128)(2,1)S(1)}, bf16[64,1024]{1,0:T(8,128)(2,1)}, u32[]{:S(2)}) copy-start(bf16[64,1024]{1,0:T(8,128)(2,1)} %vk.1) | copy-start | bytes 393220
  3.1 0.9 %copy-start.2 = (bf16[64,1024]{1,0:T(8,128)(2,1)S(1)}, bf16[64,1024]{1,0:T(8,128)(2,1)}, u32[]{:S(2)}) copy-start(bf16[64,1024]{1,0:T(8,128)(2,1)} %vv.1) | copy-start | bytes 393220
  4.0 0.8 %copy-start.3 = (bf16[64,512]{1,0:T(8,128)(2,1)S(1)}, bf16[64,512]{1,0:T(8,128)(2,1)}, u32[]{:S(2)}) copy-start(bf16[64,512]{1,0:T(8,128)(2,1)} %vcq.1) | copy-start | bytes 196612
  4.9 0.8 %copy-start.4 = (bf16[16,1024]{1,0:T(8,128)(2,1)S(1)}, bf16[16,1024]{1,0:T(8,128)(2,1)}, u32[]{:S(2)}) copy-start(bf16[16,1024]{1,0:T(8,128)(2,1)} %acq.1) | copy-start | bytes 98308
  5.6 0.7 %copy-start.5 = (bf16[16,512]{1,0:T(8,128)(2,1)S(1)}, bf16[16,512]{1,0:T(8,128)(2,1)}, u32[]{:S(2)}) copy-start(bf16[16,512]{1,0:T(8,128)(2,1)} %aq.1) | copy-start | bytes 49156
  6.3 0.7 %copy-start.6 = (bf16[16,512]{1,0:T(8,128)(2,1)S(1)}, bf16[16,512]{1,0:T(8,128)(2,1)}, u32[]{:S(2)}) copy-start(bf16[16,512]{1,0:T(8,128)(2,1)} %ak.1) | copy-start | bytes 49156
  7.1 0.7 %copy-start.7 = (bf16[16,512]{1,0:T(8,128)(2,1)S(1)}, bf16[16,512]{1,0:T(8,128)(2,1)}, u32[]{:S(2)}) copy-start(bf16[16,512]{1,0:T(8,128)(2,1)} %av.1) | copy-start | bytes 49156

commit v2 on v1

--- a/solution.py
+++ b/solution.py
@@ -126,9 +126,6 @@
         c.wait()
     pl.semaphore_wait(barrier, n - 1)
 
-    order = sorted(range(1, n), key=lambda k: abs(k - half))
-    near = list(range(1, half))
-
     def lanes(ref, rows, block):
         return ref.at[rows, pl.ds(pl.multiple_of(block * LANES, LANES), LANES)]
 
@@ -144,18 +141,22 @@
     def drain(ref, sem):
         pltpu.make_async_copy(ref, ref, sem).wait()
 
-    everyone = [lax.rem(me + k, n) for k in order]
-    halfmates = [my_half * half + lax.rem(my_pair + k, half) for k in near]
+    other = (1 - my_half) * half
+    far_peers = [other + lax.rem(my_pair + k, half) for k in range(half)]
+    near_peers = [my_half * half + lax.rem(my_pair + k, half) for k in range(1, half)]
+    everyone = far_peers + near_peers
 
     kv, qa = pl.ds(0, kv_rows), pl.ds(kv_rows, v_rows - kv_rows)
+    for peers in (far_peers, near_peers):
+        for rows, kind in ((kv, KV), (qa, QA)):
+            for peer in peers:
+                remote(lanes(vstage, rows, peer), vrecv.at[me, rows], kind, peer)
     for rows, kind in ((kv, KV), (qa, QA)):
-        for peer in everyone:
-            remote(lanes(vstage, rows, peer), vrecv.at[me, rows], kind, peer)
         local(lanes(vstage, rows, me), vrecv.at[me, rows], kind)
     for peer in everyone:
         remote(lanes(astage, slice(None), lax.rem(peer, half)), arecv.at[me], AU, peer)
     local(lanes(astage, slice(None), my_pair), arecv.at[me], AU)
-    for peer in halfmates:
+    for peer in near_peers:
         remote(lanes(cstage, slice(None), lax.rem(peer, half)), crecv.at[my_pair], CQ, peer)
     local(lanes(cstage, slice(None), my_pair), crecv.at[my_pair], CQ)
 
@@ -189,7 +190,7 @@
         low,
     )
     as_buf[...] = states.reshape(n, at, LANES)
-    for peer in halfmates:
+    for peer in near_peers:
         remote(as_buf.at[peer], lanes(o_as, slice(None), my_pair), OAS, peer)
     local(as_buf.at[me], lanes(o_as, slice(None), my_pair), OAS)
 
@@ -207,7 +208,7 @@
     drain(crecv, recv_sem.at[CQ])
     q = crecv[...].reshape(half * vt, LANES)
     vc_buf[...] = head_pair(q, normed, states, low).reshape(half, vt, LANES)
-    for peer in halfmates:
+    for peer in near_peers:
         remote(vc_buf.at[lax.rem(peer, half)], lanes(o_vc, slice(None), my_pair), OVC, peer)
     local(vc_buf.at[my_pair], lanes(o_vc, slice(None), my_pair), OVC)
 
@@ -226,6 +227,15 @@
     drain(o_ac, recv_sem.at[OAC])
 
 
+def hand_over(*refs):
+    sems = refs[8]
+    copies = [pltpu.make_async_copy(refs[i], refs[4 + i], sems.at[i]) for i in range(4)]
+    for c in copies:
+        c.start()
+    for c in copies:
+        c.wait()
+
+
 def exchanged_shards(
     n, video_q, video_k, video_v, audio_q, audio_k, audio_v,
     video_cross_q, audio_cross_q, audio_key_gain, video_key_gain,
@@ -236,11 +246,11 @@
     anywhere = pl.BlockSpec(memory_space=pl.ANY)
     vmem = pl.BlockSpec(memory_space=pltpu.VMEM)
     outs = [video_q, audio_q, video_cross_q, audio_cross_q]
-    return pl.pallas_call(
+    results = pl.pallas_call(
         functools.partial(kernel, n, vt, at),
-        out_shape=[jax.ShapeDtypeStruct(x.shape, bf) for x in outs],
+        out_shape=[pltpu.VMEM(x.shape, bf) for x in outs],
         in_specs=[anywhere] * 8 + [vmem] * 2,
-        out_specs=[anywhere] * 4,
+        out_specs=[vmem] * 4,
         scratch_shapes=[
             pltpu.VMEM((3 * vt + at, video_q.shape[1]), bf),
             pltpu.VMEM((3 * at, audio_q.shape[1]), bf),
@@ -257,12 +267,19 @@
             pltpu.SemaphoreType.DMA((8,)),
         ],
         compiler_params=pltpu.CompilerParams(
-            collective_id=0, has_side_effects=True, vmem_limit_bytes=32 * 2**20
+            collective_id=0, has_side_effects=True, vmem_limit_bytes=60 * 2**20
         ),
     )(
         video_q, video_k, video_v, audio_q, audio_k, audio_v, video_cross_q, audio_cross_q,
         audio_key_gain.reshape(1, AHEAD), video_key_gain.reshape(1, VHEAD),
     )
+    return pl.pallas_call(
+        hand_over,
+        out_shape=[jax.ShapeDtypeStruct(x.shape, bf) for x in outs],
+        in_specs=[vmem] * 4,
+        out_specs=[anywhere] * 4,
+        scratch_shapes=[pltpu.SemaphoreType.DMA((4,))],
+    )(*[pltpu.with_memory_space_constraint(r, pltpu.VMEM) for r in results])
 
 
 def solution(mesh):

time: 36.4 us -> 27 us (0.74)
  local copies, waits for them, and re-layouts: 9.62 us -> 0 us
  Pallas kernels: 25.6 us -> 26.1 us
    unnamed x24 -> x0, local copies, waits for them, and re-layouts: 9.62 us -> none
    pallas_call x1 -> x2, Pallas kernels: 25.6 us -> 26.1 us  [the longest x1 25.4 us: exchanged_shards(): pl.pallas_call(functools.partial(kernel, n, vt, at), out_shape=[pltpu.VME...]
where the time goes in v2:
time: 27 us; the launch traced here: 26.8 us
  Pallas kernels  26.1 us (97%)
  between operations  0.64 us (2%)
    pallas_call x1, Pallas kernels, exchanged_shards(): pl.pallas_call(functools.partial(kernel, n, vt, at), out_shape=[pltpu.VME...  25.4 us
    pallas_call x1, Pallas kernels, exchanged_shards(): pl.pallas_call(hand_over, out_shape=[jax.ShapeDtypeStruct(x.shape, bf) fo...  0.72 us

profile of v2, /device:TPU:0, one launch (start us, length us, event | category | flops | bytes accessed | tf_op | source)
XLA Modules:
  0.0 26.8 jit_solution(45205113678898069)
XLA Ops:
  0.6 25.4 %shard_map.129 = (bf16[64,1024]{1,0:T(8,128)(2,1)S(1)}, bf16[16,512]{1,0:T(8,128)(2,1)S(1)}, bf16[64,512]{1,0:T(8,128)(2,1)S(1)}, bf16[16,1024]{1,0:T(8,128)(2,1)S(1)}) custom-call(bf16[64,1024]{1,0:T(8,128)(2,1)} %vq.1, bf16[64,1024]{1,0:T(8,128)(2,1)} %vk.1, bf16[64,1024]{1,0:T(8,128)(2,1)} %vv.1, bf16[16,512]{1,0:T(8,128)(2,1)} %aq.1, ...), custom_call_target="tpu_custom_call" | custom-call | tf_op jit(solution)/shard_map/pallas_call | solution.py:249
  26.1 0.7 %shard_map.130 = (bf16[64,1024]{1,0:T(8,128)(2,1)}, bf16[16,512]{1,0:T(8,128)(2,1)}, bf16[64,512]{1,0:T(8,128)(2,1)}, bf16[16,1024]{1,0:T(8,128)(2,1)}) custom-call(bf16[64,1024]{1,0:T(8,128)(2,1)S(1)} %get-tuple-element.8.refs_0_, bf16[16,512]{1,0:T(8,128)(2,1)S(1)} %get-tuple-element.9.refs_1_, bf16[64,512]{1,0:T(8,128)(2,1)S(1)} %get-tuple-element.10.refs_2_, ...), custom_call_target="tpu_custom_call" | custom-call | tf_op jit(solution)/shard_map/pallas_call | solution.py:276

commit v3 on v2

--- a/solution.py
+++ b/solution.py
@@ -92,8 +92,8 @@
     n, vt, at,
     vq, vk, vv, aq, ak, av, vcq, acq, again, vgain,
     o_vs, o_as, o_vc, o_ac,
-    vstage, astage, cstage, vrecv, arecv, crecv, vs_buf, as_buf, vc_buf, ac_buf,
-    stage_sem, send_sem, recv_sem,
+    vstage, astage, cstage, vrecv, arecv, crecv, vs_buf, as_buf, vc_buf, ac_buf, key_buf,
+    stage_sem, send_sem, recv_sem, query_sem,
 ):
     me = lax.axis_index("seq")
     half = n // 2
@@ -113,9 +113,6 @@
         (vcq, cstage),
     ]
     stages = [pltpu.make_async_copy(s, d, stage_sem.at[i]) for i, (s, d) in enumerate(stages)]
-    for c in stages:
-        c.start()
-
     barrier = pltpu.get_barrier_semaphore()
     for k in range(1, n):
         pl.semaphore_signal(
@@ -123,6 +120,8 @@
             device_id_type=pl.DeviceIdType.MESH,
         )
     for c in stages:
+        c.start()
+    for c in stages[:2]:
         c.wait()
     pl.semaphore_wait(barrier, n - 1)
 
@@ -147,12 +146,18 @@
     everyone = far_peers + near_peers
 
     kv, qa = pl.ds(0, kv_rows), pl.ds(kv_rows, v_rows - kv_rows)
-    for peers in (far_peers, near_peers):
-        for rows, kind in ((kv, KV), (qa, QA)):
-            for peer in peers:
-                remote(lanes(vstage, rows, peer), vrecv.at[me, rows], kind, peer)
-    for rows, kind in ((kv, KV), (qa, QA)):
-        local(lanes(vstage, rows, me), vrecv.at[me, rows], kind)
+    for peer in everyone:
+        remote(lanes(vstage, kv, peer), vrecv.at[me, kv], KV, peer)
+    local(lanes(vstage, kv, me), vrecv.at[me, kv], KV)
+    for c in stages[2:]:
+        c.wait()
+    pltpu.make_async_copy(lanes(vstage, qa, me), vrecv.at[me, qa], query_sem.at[me]).start()
+    for peer in everyone:
+        pltpu.make_async_remote_copy(
+            src_ref=lanes(vstage, qa, peer), dst_ref=vrecv.at[me, qa],
+            send_sem=send_sem.at[QA], recv_sem=query_sem.at[me],
+            device_id={"seq": peer}, device_id_type=pl.DeviceIdType.MESH,
+        ).start()
     for peer in everyone:
         remote(lanes(astage, slice(None), lax.rem(peer, half)), arecv.at[me], AU, peer)
     local(lanes(astage, slice(None), my_pair), arecv.at[me], AU)
@@ -161,22 +166,32 @@
     local(lanes(cstage, slice(None), my_pair), crecv.at[my_pair], CQ)
 
     drain(vrecv.at[:, kv], recv_sem.at[KV])
-    drain(vrecv.at[:, qa], recv_sem.at[QA])
     key_rows = vrecv[:, :vt].reshape(n * vt, VHEAD)
     value_rows = vrecv[:, vt : 2 * vt].reshape(n * vt, VHEAD)
-    for i in range(0, n, 2):
-        q = vrecv[i : i + 2, 2 * vt : 3 * vt].reshape(2 * vt, VHEAD)
-        vs_buf[i : i + 2] = one_head(q, key_rows, value_rows).reshape(2, vt, VHEAD)
-    for peer in everyone:
-        remote(vs_buf.at[peer], lanes(o_vs, slice(None), me), OVS, peer)
-    local(vs_buf.at[me], lanes(o_vs, slice(None), me), OVS)
-
-    states = vs_buf[...].reshape(n * vt, VHEAD)
-    x = states.astype(jnp.float32)
-    factor = lax.rsqrt(jnp.sum(x * x, axis=1, keepdims=True) * (1.0 / VHEAD) + 1e-06)
-    normed = (x * factor * vgain[...]).astype(jnp.bfloat16)
+    arrivals = [base + lax.rem(my_pair - k + half, half) for base in (my_half * half, other) for k in range(half)]
+    own = arrivals[0]
+    for first, second in zip(arrivals[::2], arrivals[1::2]):
+        pair = (first, second)
+        for source in pair:
+            drain(vrecv.at[source, qa], query_sem.at[source])
+        q = jnp.concatenate([vrecv[source, 2 * vt : 3 * vt] for source in pair], axis=0)
+        states = one_head(q, key_rows, value_rows)
+        for source, rows in zip(pair, (states[:vt], states[vt:])):
+            vs_buf[source] = rows
+        x = states.astype(jnp.float32)
+        factor = lax.rsqrt(jnp.sum(x * x, axis=1, keepdims=True) * (1.0 / VHEAD) + 1e-06)
+        normed = (x * factor * vgain[...]).astype(jnp.bfloat16)
+        for source, rows in zip(pair, (normed[:vt], normed[vt:])):
+            key_buf[source] = rows
+        for source in pair:
+            if source is own:
+                local(vs_buf.at[me], lanes(o_vs, slice(None), me), OVS)
+            else:
+                remote(vs_buf.at[source], lanes(o_vs, slice(None), me), OVS, source)
+
     q = vrecv[:, 3 * vt :].reshape(n * at, VHEAD)
-    ac_buf[...] = one_head(q, normed, states).reshape(n, at, VHEAD)
+    keys, states = key_buf[...].reshape(n * vt, VHEAD), vs_buf[...].reshape(n * vt, VHEAD)
+    ac_buf[...] = one_head(q, keys, states).reshape(n, at, VHEAD)
     for peer in everyone:
         remote(ac_buf.at[peer], lanes(o_ac, slice(None), me), OAC, peer)
     local(ac_buf.at[me], lanes(o_ac, slice(None), me), OAC)
@@ -262,9 +277,11 @@
             pltpu.VMEM((n, at, LANES), bf),
             pltpu.VMEM((half, vt, LANES), bf),
             pltpu.VMEM((n, at, LANES), bf),
+            pltpu.VMEM((n, vt, LANES), bf),
             pltpu.SemaphoreType.DMA((8,)),
             pltpu.SemaphoreType.DMA((8,)),
             pltpu.SemaphoreType.DMA((8,)),
+            pltpu.SemaphoreType.DMA((n,)),
         ],
         compiler_params=pltpu.CompilerParams(
             collective_id=0, has_side_effects=True, vmem_limit_bytes=60 * 2**20

time: 27 us -> 26.3 us (0.974)
  Pallas kernels: 26.1 us -> 25.5 us
    pallas_call x1, Pallas kernels: 25.4 us -> 24.8 us  [exchanged_shards(): pl.pallas_call(functools.partial(kernel, n, vt, at), out_shape=[pltpu.VME...]
where the time goes in v3:
time: 26.3 us; the launch traced here: 26.1 us
  Pallas kernels  25.5 us (97%)
  between operations  0.64 us (2%)
    pallas_call x1, Pallas kernels, exchanged_shards(): pl.pallas_call(functools.partial(kernel, n, vt, at), out_shape=[pltpu.VME...  24.8 us
    pallas_call x1, Pallas kernels, exchanged_shards(): pl.pallas_call(hand_over, out_shape=[jax.ShapeDtypeStruct(x.shape, bf) fo...  0.72 us

profile of v3, /device:TPU:0, one launch (start us, length us, event | category | flops | bytes accessed | tf_op | source)
XLA Modules:
  0.0 26.1 jit_solution(3948383769398198067)
XLA Ops:
  0.6 24.8 %shard_map.129 = (bf16[64,1024]{1,0:T(8,128)(2,1)S(1)}, bf16[16,512]{1,0:T(8,128)(2,1)S(1)}, bf16[64,512]{1,0:T(8,128)(2,1)S(1)}, bf16[16,1024]{1,0:T(8,128)(2,1)S(1)}) custom-call(bf16[64,1024]{1,0:T(8,128)(2,1)} %vq.1, bf16[64,1024]{1,0:T(8,128)(2,1)} %vk.1, bf16[64,1024]{1,0:T(8,128)(2,1)} %vv.1, bf16[16,512]{1,0:T(8,128)(2,1)} %aq.1, ...), custom_call_target="tpu_custom_call" | custom-call | tf_op jit(solution)/shard_map/pallas_call | solution.py:264
  25.4 0.7 %shard_map.130 = (bf16[64,1024]{1,0:T(8,128)(2,1)}, bf16[16,512]{1,0:T(8,128)(2,1)}, bf16[64,512]{1,0:T(8,128)(2,1)}, bf16[16,1024]{1,0:T(8,128)(2,1)}) custom-call(bf16[64,1024]{1,0:T(8,128)(2,1)S(1)} %get-tuple-element.8.refs_0_, bf16[16,512]{1,0:T(8,128)(2,1)S(1)} %get-tuple-element.9.refs_1_, bf16[64,512]{1,0:T(8,128)(2,1)S(1)} %get-tuple-element.10.refs_2_, ...), custom_call_target="tpu_custom_call" | custom-call | tf_op jit(solution)/shard_map/pallas_call | solution.py:293
